TPU v7x, 256 devices: a whole 4x4x8 slice. The times are simulated.
256 devices in a mesh: wide: 32 (over y, x, core), rep: 8 (over z).
Axes of the slice: x: 4, y: 4, z: 8, core: 2. Of those that a mesh axis runs over, the one named last changes fastest.
Arguments:
- queries: bfloat16 [2048, 128, 576], P(('rep', 'wide')), parts along dimension 0, may hold values from -16 to 16
- latent_cache: bfloat16 [2048, 384, 576], P(('rep', 'wide')), parts along dimension 0, may hold values from -4 to 4
- lengths: int32 [2048], P(('rep', 'wide')), parts along dimension 0, may hold values from 1 to 384, as said below
- occupied: int32 [2048], P(('rep', 'wide')), parts along dimension 0, may hold values 0 or 1
- residual: bfloat16 [2048, 3584], P(('rep', 'wide')), parts along dimension 0, may hold values from -4 to 4
- w_uv: bfloat16 [128, 512, 128], P('wide'), may hold values from -0.25 to 0.25
- w_out: bfloat16 [16384, 3584], P('wide'), may hold values from -0.046875 to 0.046875
- norm_gain: bfloat16 [3584], replicated, may hold values from 0.5 to 1.5
- w_gate: bfloat16 [3584, 9216], P(None, 'wide'), may hold values from -0.09375 to 0.09375
- w_up: bfloat16 [3584, 9216], P(None, 'wide'), may hold values from -0.09375 to 0.09375
- w_down: bfloat16 [9216, 3584], P('wide'), may hold values from -0.0625 to 0.0625
Outputs:
- layer_out: bfloat16 [2048, 3584], P(('rep', 'wide')), parts along dimension 0
There are 8 independent parts, one for each index of `rep`. A program takes and returns all parts, laid end to end along the dimension named above; an argument that names none is the same for every part. Nothing has to cross between parts.
Inputs may be any that keep to these rules, and one draw needn't show every extreme that they name: `lengths`: some slot has length 384 in every draw.
All inputs are finite; a program needn't handle non-finite values. No bound on the sum of `occupied` on one device may be relied on, other than what follows from the above.
Results may differ from a plain program's by a relative error of at most 0.009.
Values may be sent and summed in bfloat16 or wider, within the bound.
A program may use at most 64 MiB of HBM per device.

v0:
```python
import jax
import jax.numpy as jnp
from jax import lax
from jax.sharding import PartitionSpec as P

softmax_scale = 192.0 ** (-0.5)


def norm_rows(hidden, norm_gain):
    hidden_f = hidden.astype(jnp.float32)
    inverse = lax.rsqrt(jnp.mean(hidden_f * hidden_f, axis=1, keepdims=True) + 1e-06)
    return (hidden_f * inverse * norm_gain.astype(jnp.float32)).astype(jnp.bfloat16)


def expand_rows(normed, w_gate, w_up):
    gate = jnp.dot(normed, w_gate, preferred_element_type=jnp.float32)
    upper = jnp.dot(normed, w_up, preferred_element_type=jnp.float32)
    return (jax.nn.silu(gate) * upper).astype(jnp.bfloat16)


def shards(
    queries, latent_cache, lengths, occupied, residual, w_uv, w_out, norm_gain, w_gate, w_up, w_down
):
    slot_count = queries.shape[0]
    positions = latent_cache.shape[1]
    latent = w_uv.shape[1]
    scores = (
        jnp.einsum("shc,sjc->shj", queries, latent_cache, preferred_element_type=jnp.float32)
        * softmax_scale
    )
    live = lax.broadcasted_iota(jnp.int32, (slot_count, positions), 1) < lengths[:, None]
    live = live[:, None, :]
    scores = jnp.where(live, scores, jnp.float32(-1e30))
    peak = jnp.max(scores, axis=2, keepdims=True)
    weights = jnp.where(live, jnp.exp(scores - peak), jnp.float32(0.0))
    probs = (weights / jnp.sum(weights, axis=2, keepdims=True)).astype(jnp.bfloat16)
    result = jnp.einsum(
        "shj,sjc->shc", probs, latent_cache[:, :, :latent], preferred_element_type=jnp.float32
    )
    latent_out = (result * occupied.astype(jnp.float32)[:, None, None]).astype(jnp.bfloat16)
    by_head = lax.all_to_all(latent_out, "wide", split_axis=1, concat_axis=0, tiled=True)
    all_rows = by_head.shape[0]
    values = jnp.einsum("shc,hcv->shv", by_head, w_uv, preferred_element_type=jnp.float32).astype(
        jnp.bfloat16
    )
    values = values.reshape(all_rows, -1)
    picked = values
    summed = lax.psum_scatter(
        jnp.dot(picked, w_out, preferred_element_type=jnp.float32),
        "wide",
        scatter_dimension=0,
        tiled=True,
    )
    hidden = (summed + residual.astype(jnp.float32)).astype(jnp.bfloat16)
    normed = norm_rows(hidden, norm_gain)
    act = expand_rows(lax.all_gather(normed, "wide", axis=0, tiled=True), w_gate, w_up)
    picked = act
    ffn = lax.psum_scatter(
        jnp.dot(picked, w_down, preferred_element_type=jnp.float32),
        "wide",
        scatter_dimension=0,
        tiled=True,
    )
    return (hidden.astype(jnp.float32) + ffn).astype(jnp.bfloat16)


def solution(mesh):
    in_specs = (
        P(("rep", "wide"), None, None),
        P(("rep", "wide"), None, None),
        P(("rep", "wide")),
        P(("rep", "wide")),
        P(("rep", "wide"), None),
        P("wide", None, None),
        P("wide", None),
        P(),
        P(None, "wide"),
        P(None, "wide"),
        P("wide", None),
    )
    out_specs = P(("rep", "wide"), None)
    return jax.shard_map(shards, mesh=mesh, in_specs=in_specs, out_specs=out_specs, check_vma=False)
```

profile of v0, /device:TPU:1, one launch (start us, length us, event | category | flops | bytes accessed | tf_op | source)
XLA Modules:
  0.0 289.4 jit_solution(15779915940135867512)
XLA Ops:
  6.5 0.0 copy-start
  6.5 0.0 reduce-scatter.3.cloned.1.call-start
  6.5 0.8 convert_element_type.38
  7.3 0.7 iota_compare_fusion
  8.1 4.8 %fusion.22 = (f32[8,128]{1,0:T(8,128)S(1)}, f32[8,128,384]{2,1,0:T(8,128)}) fusion(pred[8,384]{1,0:T(8,128)(4,1)S(1)} %iota_compare_fusion, bf16[8,128,576]{1,2,0:T(8,128)(2,1)} %param.11, bf16[8,384,576]{1,2,0:T(8,128)(2,1)} %param.12), kind=kOutput, calls=%fused_computation.32 | convolution fusion | flops 454951296 | bytes 6298624 | tf_op jit(solution)/shard_map/sub | solution.py:35
  12.9 3.5 %multiply_convert_fusion = bf16[8,128,512]{2,1,0:T(8,128)(2,1)S(1)} fusion(bf16[8,384,576]{1,2,0:T(8,128)(2,1)} %param.12, f32[8]{0:T(128)S(1)} %convert_element_type.38, f32[8,128,384]{2,1,0:T(8,128)} %get-tuple-element.8, f32[8,128]{1,0:T(8,128)S(1)} %get-tuple-element.7), kind=kOutput, calls=%fused_computation.3 | convolution fusion | flops 404488192 | bytes 5771296 | tf_op jit(solution)/shard_map/shj,sjc->shc/dot_general | solution.py:37
  16.4 0.0 copy-start.4
  16.4 0.6 copy.16
  17.0 0.0 copy-start.1
  17.0 25.8 %all_to_all.18 = bf16[8,128,512]{2,0,1:T(8,128)(2,1)S(1)} all-to-all(bf16[8,128,512]{2,0,1:T(8,128)(2,1)S(1)} %copy.16), channel_id=1, replica_groups=mesh['wide'=32,'rep'=8] {'wide'}, dimensions={1} | all-to-all | bytes 2097152 | tf_op jit(solution)/shard_map/all_to_all | solution.py:41
  42.8 0.0 copy-done.4
  42.8 0.5 convolution_convert_fusion
  43.3 0.0 copy-done.1
  43.3 2.9 %fusion.23 = f32[256,3584]{1,0:T(8,128)} fusion(bf16[256,512]{0,1:T(8,128)(2,1)S(1)} %bitcast.20, bf16[512,3584]{1,0:T(8,128)(2,1)S(1)} %copy-done.1), kind=kOutput, calls=%fused_computation.33 | convolution fusion | flops 939524096 | bytes 7602176 | tf_op jit(solution)/shard_map/dot_general | solution.py:49
  46.3 0.0 copy-start.3
  46.3 0.0 copy-start.2
  46.3 0.0 reduce-scatter.3.cloned.1.call-update
  46.3 0.0 all-gather.2.cloned.1.call-start
  46.4 0.6 copy-done.3
  47.0 85.6 %reduce-scatter.3.cloned.1.call-done = f32[8,3584]{1,0:T(8,128)} async-done(((f32[256,3584]{1,0:T(8,128)}), f32[8,3584]{1,0:T(8,128)}) %reduce-scatter.3.cloned.1.call-update) | async-done | bytes 114704 | tf_op jit(solution)/shard_map/reduce_scatter | solution.py:48
  132.6 0.0 copy-done.2
  132.6 1.0 fusion.17
  133.6 0.7 fusion.19
  134.3 0.0 all-gather.2.cloned.1.call-update
  134.4 0.0 reduce-scatter.5.cloned.1.call-start
  134.4 51.1 %all-gather.2.cloned.1.call-done = bf16[256,3584]{1,0:T(8,128)(2,1)} async-done(((bf16[8,3584]{1,0:T(8,128)(2,1)}), bf16[256,3584]{1,0:T(8,128)(2,1)}) %all-gather.2.cloned.1.call-update) | async-done | bytes 1835024 | tf_op jit(solution)/shard_map/all_gather | solution.py:56
  185.5 2.9 fusion.24
  188.3 0.0 copy-done
  188.4 6.8 %fusion.7 = f32[256,3584]{1,0:T(8,128)} fusion(bf16[288,3584]{1,0:T(8,128)(2,1)S(1)} %copy-done, bf16[256,3584]{1,0:T(8,128)(2,1)} %all-gather.2.cloned.1.call-done, bf16[3584,288]{0,1:T(8,128)(2,1)} %param.20, f32[256,288]{0,1:T(8,128)S(1)} %fusion.24), kind=kOutput, calls=%fused_computation.11 | convolution fusion | flops 1057406976 | bytes 9928704 | tf_op jit(solution)/shard_map/dot_general | solution.py:59
  195.2 0.0 reduce-scatter.5.cloned.1.call-update
  195.2 86.1 %reduce-scatter.5.cloned.1.call-done = f32[8,3584]{1,0:T(8,128)} async-done(((f32[256,3584]{1,0:T(8,128)}), f32[8,3584]{1,0:T(8,128)}) %reduce-scatter.5.cloned.1.call-update) | async-done | bytes 114704 | tf_op jit(solution)/shard_map/reduce_scatter | solution.py:58
  281.3 1.5 fusion.20
  (2 shorter events, 0.0 us)
Async XLA Ops:
  6.5 181.8 %copy-start = (bf16[288,3584]{1,0:T(8,128)(2,1)S(1)}, bf16[288,3584]{1,0:T(8,128)(2,1)}, u32[]{:S(2)}) copy-start(bf16[288,3584]{1,0:T(8,128)(2,1)} %param.21) | copy-start | bytes 6193156
  6.5 126.0 %reduce-scatter.3.cloned.1.call-start = ((), (), s32[]{:S(2)}) async-start(), calls=%async_computation.3 | async-start | bytes 3784704 | tf_op jit(solution)/shard_map/reduce_scatter | solution.py:48
  16.4 26.4 %copy-start.4 = (bf16[4,512,128]{2,1,0:T(8,128)(2,1)S(1)}, bf16[4,512,128]{2,1,0:T(8,128)(2,1)}, u32[]{:S(2)}) copy-start(bf16[4,512,128]{2,1,0:T(8,128)(2,1)} %param.16) | copy-start | bytes 1572868
  17.0 26.3 %copy-start.1 = (bf16[512,3584]{1,0:T(8,128)(2,1)S(1)}, bf16[512,3584]{1,0:T(8,128)(2,1)}, u32[]{:S(2)}) copy-start(bf16[512,3584]{1,0:T(8,128)(2,1)} %param.17) | copy-start | bytes 11010052
  46.3 0.7 copy-start.3
  46.3 86.3 %copy-start.2 = (bf16[8,3584]{1,0:T(8,128)(2,1)S(1)}, bf16[8,3584]{1,0:T(8,128)(2,1)}, u32[]{:S(2)}) copy-start(bf16[8,3584]{1,0:T(8,128)(2,1)} %param.15) | copy-start | bytes 172036
  46.3 139.2 %all-gather.2.cloned.1.call-start = ((), (), s32[]{:S(2)}) async-start(), calls=%async_computation.4 | async-start | bytes 1892352 | tf_op jit(solution)/shard_map/all_gather | solution.py:56
  134.4 146.9 %reduce-scatter.5.cloned.1.call-start = ((), (), s32[]{:S(2)}) async-start(), calls=%async_computation.5 | async-start | bytes 3784704 | tf_op jit(solution)/shard_map/reduce_scatter | solution.py:58
Sparse Core Ops, SparseCore 0:
  46.4 86.0 reduce-scatter.2
  135.4 50.0 all-gather.1
  195.3 85.9 reduce-scatter.4
where the time goes:
time: 290 us; the launch traced here: 289 us
  waiting for transfers between devices  223 us (77%)
  blocking collectives  25.8 us (9%)
  matrix products  21.4 us (7%)
  between operations  13.2 us (5%)
  other arithmetic  4.83 us (2%)
    reduce_scatter x1, waiting for transfers between devices, shards(): lax.psum_scatter(jnp.dot(picked, w_down, preferred_element_type=jnp.float...  86.1 us
    reduce_scatter x1, waiting for transfers between devices, shards(): lax.psum_scatter(jnp.dot(picked, w_out, preferred_element_type=jnp.float3...  85.6 us
    all_gather x1, waiting for transfers between devices, shards(): lax.all_gather(normed, 'wide', axis=0, tiled=True)  51.1 us
    all_to_all x1, blocking collectives, shards(): lax.all_to_all(latent_out, 'wide', split_axis=1, concat_axis=0, tiled=True)  25.8 us
    dot_general x1, matrix products, shards(): jnp.dot(picked, w_down, preferred_element_type=jnp.float32)  6.84 us
  transfers between devices with their start and end apart: 3, of which 3 were waited for; matrix products, arithmetic and copies ran while one was open for 0% of the time, Pallas kernels for 0%

commit v1 on v0

v1 whole, which is shorter than its diff:
```python
import functools

import jax
import jax.numpy as jnp
from jax import lax
from jax.experimental import pallas as pl
from jax.experimental.pallas import tpu as pltpu
from jax.sharding import PartitionSpec as P

MESH = pl.DeviceIdType.MESH
F32 = jnp.float32
BF16 = jnp.bfloat16
softmax_scale = 192.0 ** (-0.5)

SIDE = 4
CHIPS = SIDE * SIDE
DEVICES = 2 * CHIPS
SLOT = 8
HEADS = 128
OWN_HEADS = HEADS // DEVICES
LAT = 512
KEY = 576
LMAX = 384
D = 3584
HALF = D // 2
PART = HALF // 2
ROWS = DEVICES * SLOT
FFS = 288
NT = (((1,), (1,)), ((), ()))
TN = (((0,), (0,)), ((), ()))


def remote(src, dst, send, recv, to):
    return pltpu.make_async_remote_copy(
        src_ref=src,
        dst_ref=dst,
        send_sem=send,
        recv_sem=recv,
        device_id={"wide": to},
        device_id_type=MESH,
    )


def layer_kernel(
    lengths,
    occupied,
    queries,
    cache,
    w_uv,
    w_out,
    w_gate,
    w_up,
    w_down,
    residual,
    gain,
    out,
    q_v,
    c_v,
    uv_v,
    wo_v,
    gu_v,
    wd_v,
    load_sem,
    attn,
    a2a_out,
    a2a_in,
    a2a_send,
    a2a_recv,
    rowvals,
    values,
    acc,
    p0,
    r0,
    s0,
    r1,
    s1,
    r2,
    rs_send,
    rs_recv,
    res_own,
    res16,
    hid,
    sq_own,
    sq_in,
    gathered,
    ag_send,
    ag_recv,
    last_own,
    last_in,
    pair_send,
    pair_recv,
):
    me = lax.axis_index("wide")
    core = lax.rem(me, 2)
    chip = me // 2
    x = lax.rem(chip, SIDE)
    y = chip // SIDE
    partner = me + 1 - 2 * core

    def at(cy, cx):
        return (cy * SIDE + cx) * 2 + core

    def along_x(k):
        return lax.rem(x + k, SIDE)

    def along_y(k):
        return lax.rem(y + k, SIDE)

    loads = []

    def load(src, dst):
        copy = pltpu.make_async_copy(src, dst, load_sem.at[len(loads)])
        copy.start()
        loads.append(copy)
        return copy

    slot_loads = []
    for s in range(SLOT):
        slot_loads.append((load(queries.at[s], q_v.at[s]), load(cache.at[s], c_v.at[s])))
    uv_loads = [
        load(w_uv.at[h], uv_v.at[:, pl.ds(h * 128, 128)]) for h in range(OWN_HEADS)
    ]
    wo_loads = [load(w_out.at[:, pl.ds(j * HALF, HALF)], wo_v.at[j]) for j in range(2)]
    gu_loads = [
        load(w_gate, gu_v.at[pl.ds(0, FFS)]),
        load(w_up, gu_v.at[pl.ds(FFS, FFS)]),
    ]
    wd_loads = [load(w_down.at[:, pl.ds(j * HALF, HALF)], wd_v.at[j]) for j in range(2)]

    barrier = pltpu.get_barrier_semaphore()

    def greet(k, carry):
        pl.semaphore_signal(
            barrier, inc=1, device_id={"wide": lax.rem(me + k, DEVICES)}, device_id_type=MESH
        )
        return carry

    lax.fori_loop(1, DEVICES, greet, 0)

    position = lax.broadcasted_iota(jnp.int32, (HEADS, LMAX), 1)
    for s in range(SLOT):
        for copy in slot_loads[s]:
            copy.wait()
        keys = c_v[s]
        scores = lax.dot_general(q_v[s], keys, TN, preferred_element_type=F32)
        scores = jnp.where(position < lengths[s], scores, F32(-1e30))
        peak = jnp.max(scores, axis=1, keepdims=True)
        weights = jnp.exp((scores - peak) * F32(softmax_scale))
        flag = occupied[s].astype(F32)
        probs = (weights * (flag / jnp.sum(weights, axis=1, keepdims=True))).astype(BF16)
        result = lax.dot_general(probs, keys[:LAT], NT, preferred_element_type=F32)
        for lane in range(LAT // 128):
            attn[lane, s * HEADS : (s + 1) * HEADS, :] = result[:, lane * 128 : (lane + 1) * 128]

    def pack(d, carry):
        for pair in range(OWN_HEADS // 2):
            for lane in range(LAT // 128):
                rows = [
                    attn[lane, pl.ds(d * OWN_HEADS + 2 * pair + i, SLOT, stride=HEADS), :]
                    for i in range(2)
                ]
                a2a_out[d, 16 * pair : 16 * pair + 16, lane * 128 : (lane + 1) * 128] = (
                    jnp.concatenate(rows, axis=0).astype(BF16)
                )
        return carry

    lax.fori_loop(0, DEVICES, pack, 0)

    pl.semaphore_wait(barrier, DEVICES - 1)

    for j in range(2):
        res_own[j] = residual[:, j * HALF : (j + 1) * HALF].astype(F32)
    res_copy = remote(
        res_own.at[1 - core], res16.at[core], pair_send.at[0], pair_recv.at[0], partner
    )
    res_copy.start()
    res16[core] = res_own[core]

    def a2a_copy(k):
        to = lax.rem(me + k, DEVICES)
        return remote(a2a_out.at[to], a2a_in.at[me], a2a_send.at[k], a2a_recv.at[k], to)

    def a2a_start(k, carry):
        a2a_copy(k).start()
        return carry

    lax.fori_loop(1, DEVICES, a2a_start, 0)
    a2a_in[me] = a2a_out[me]
    for copy in uv_loads + wo_loads:
        copy.wait()

    def a2a_wait(k, carry):
        a2a_copy(k).wait()
        return carry

    lax.fori_loop(1, DEVICES, a2a_wait, 0)

    rowvals[...] = jnp.dot(
        a2a_in[...].reshape(DEVICES * OWN_HEADS * SLOT, LAT), uv_v[...], preferred_element_type=F32
    ).reshape(DEVICES, OWN_HEADS * SLOT, OWN_HEADS * 128)
    for h in range(OWN_HEADS):
        mine = rowvals[:, h * SLOT : (h + 1) * SLOT, h * 128 : (h + 1) * 128]
        values[:, h * 128 : (h + 1) * 128] = mine.reshape(ROWS, 128).astype(BF16)

    def reduce_scatter(n, product):
        theirs = product(1 - core)
        p0[n] = theirs.astype(BF16).reshape(CHIPS, 16, HALF)
        first = remote(p0.at[n], r0.at[n], rs_send.at[n, 0], rs_recv.at[n, 0], partner)
        first.start()
        acc[...] = product(core).reshape(CHIPS, 16, HALF)
        first.wait()

        def add(d, carry):
            s0[n, d // SIDE, lax.rem(d, SIDE)] = (acc[d] + r0[n, d].astype(F32)).astype(BF16)
            return carry

        lax.fori_loop(0, CHIPS, add, 0)
        copies = []
        for k in (1, 3, 2):
            copies.append(
                remote(
                    s0.at[n, :, along_x(k), :, pl.ds(0, PART)],
                    r1.at[n, 0, k - 1],
                    rs_send.at[n, k],
                    rs_recv.at[n, k],
                    at(y, along_x(k)),
                )
            )
            copies.append(
                remote(
                    s0.at[n, along_y(k), :, :, pl.ds(PART, PART)],
                    r1.at[n, 1, k - 1],
                    rs_send.at[n, 3 + k],
                    rs_recv.at[n, 3 + k],
                    at(along_y(k), x),
                )
            )
        for copy in copies:
            copy.start()
        for copy in copies:
            copy.wait()
        for part in range(2):
            for i in range(SIDE):
                if part == 0:
                    total = s0[n, i, x, :, :PART]
                else:
                    total = s0[n, y, i, :, PART:]
                total = total.astype(F32)
                for k in range(3):
                    total += r1[n, part, k, i].astype(F32)
                s1[n, part, i] = total.astype(BF16)
        copies = []
        for k in (1, 3, 2):
            copies.append(
                remote(
                    s1.at[n, 0, along_y(k)],
                    r2.at[n, 0, k - 1],
                    rs_send.at[n, 6 + k],
                    rs_recv.at[n, 6 + k],
                    at(along_y(k), x),
                )
            )
            copies.append(
                remote(
                    s1.at[n, 1, along_x(k)],
                    r2.at[n, 1, k - 1],
                    rs_send.at[n, 9 + k],
                    rs_recv.at[n, 9 + k],
                    at(y, along_x(k)),
                )
            )
        for copy in copies:
            copy.start()
        for copy in copies:
            copy.wait()
        sums = []
        for part, own in ((0, y), (1, x)):
            total = s1[n, part, own].astype(F32)
            for k in range(3):
                total += r2[n, part, k].astype(F32)
            sums.append(total)
        return sums

    def attend(j):
        return jnp.dot(values[...], wo_v[j], preferred_element_type=F32)

    attended = reduce_scatter(0, attend)
    res_copy.wait()
    square = jnp.zeros((16, 1), F32)
    for part in range(2):
        mine = res16[:, :, part * PART : (part + 1) * PART].reshape(16, PART) + attended[part]
        mine = mine.astype(BF16).astype(F32)
        hid[:, part * PART : (part + 1) * PART] = mine
        square += jnp.sum(mine * mine, axis=1, keepdims=True)
    sq_own[...] = jnp.broadcast_to(square, (16, 128))
    sq_copy = remote(sq_own, sq_in, pair_send.at[1], pair_recv.at[1], partner)
    sq_copy.start()
    sq_copy.wait()
    inverse = lax.rsqrt((sq_own[:, :1] + sq_in[:, :1]) * F32(1.0 / D) + F32(1e-6))
    scaled = gain[:, pl.ds(pl.multiple_of(core * HALF, 128), HALF)].astype(F32)
    gathered[core, y, x] = (hid[...] * inverse * scaled).astype(BF16)

    def lanes(part):
        return pl.ds(part * PART, PART)

    copies = []
    for k in (1, 3, 2):
        for part, to in ((0, at(along_y(k), x)), (1, at(y, along_x(k)))):
            place = gathered.at[core, y, x, :, lanes(part)]
            copies.append(
                remote(place, place, ag_send.at[3 * part + k], ag_recv.at[3 * part + k], to)
            )
    for copy in copies:
        copy.start()
    for copy in copies:
        copy.wait()
    copies = []
    for k in (1, 3, 2):
        place = gathered.at[core, :, x, :, lanes(0)]
        copies.append(
            remote(place, place, ag_send.at[6 + k], ag_recv.at[6 + k], at(y, along_x(k)))
        )
        place = gathered.at[core, y, :, :, lanes(1)]
        copies.append(
            remote(place, place, ag_send.at[9 + k], ag_recv.at[9 + k], at(along_y(k), x))
        )
    for copy in copies:
        copy.start()
    for copy in copies:
        copy.wait()
    swap = remote(gathered.at[core], gathered.at[core], ag_send.at[0], ag_recv.at[0], partner)
    swap.start()
    for copy in gu_loads + wd_loads:
        copy.wait()

    def expand(j):
        return lax.dot_general(
            gu_v[:, pl.ds(pl.multiple_of(j * HALF, 128), HALF)],
            gathered[j].reshape(ROWS, HALF),
            NT,
            preferred_element_type=F32,
        )

    up = expand(core)
    swap.wait()
    up = up + expand(1 - core)
    gate = up[:FFS]
    act = (gate / (1.0 + jnp.exp(-gate)) * up[FFS:]).astype(BF16)

    def contract(j):
        return lax.dot_general(act, wd_v[j], TN, preferred_element_type=F32)

    ffn = reduce_scatter(1, contract)
    for part in range(2):
        total = hid[:, part * PART : (part + 1) * PART] + ffn[part]
        last_own[:, :, part * PART : (part + 1) * PART] = total.reshape(2, SLOT, PART)
    last = remote(last_own.at[1 - core], last_in, pair_send.at[2], pair_recv.at[2], partner)
    last.start()
    last.wait()
    out[:, pl.ds(pl.multiple_of(core * HALF, 128), HALF)] = last_own[core].astype(BF16)
    out[:, pl.ds(pl.multiple_of((1 - core) * HALF, 128), HALF)] = last_in[...].astype(BF16)


def shards(
    queries, latent_cache, lengths, occupied, residual, w_uv, w_out, norm_gain, w_gate, w_up, w_down
):
    hbm = pl.BlockSpec(memory_space=pl.ANY)
    vmem = pl.BlockSpec(memory_space=pltpu.VMEM)
    smem = pl.BlockSpec(memory_space=pltpu.SMEM)
    dma = pltpu.SemaphoreType.DMA
    return pl.pallas_call(
        layer_kernel,
        out_shape=jax.ShapeDtypeStruct((SLOT, D), BF16),
        in_specs=[smem, smem, hbm, hbm, hbm, hbm, hbm, hbm, hbm, vmem, vmem],
        out_specs=vmem,
        scratch_shapes=[
            pltpu.VMEM((SLOT, KEY, HEADS), BF16),
            pltpu.VMEM((SLOT, KEY, LMAX), BF16),
            pltpu.VMEM((LAT, OWN_HEADS * 128), BF16),
            pltpu.VMEM((2, OWN_HEADS * 128, HALF), BF16),
            pltpu.VMEM((2 * FFS, D), BF16),
            pltpu.VMEM((2, FFS, HALF), BF16),
            dma((2 * SLOT + OWN_HEADS + 6,)),
            pltpu.VMEM((LAT // 128, SLOT * HEADS, 128), F32),
            pltpu.VMEM((DEVICES, OWN_HEADS * SLOT, LAT), BF16),
            pltpu.VMEM((DEVICES, OWN_HEADS * SLOT, LAT), BF16),
            dma((DEVICES,)),
            dma((DEVICES,)),
            pltpu.VMEM((DEVICES, OWN_HEADS * SLOT, OWN_HEADS * 128), F32),
            pltpu.VMEM((ROWS, OWN_HEADS * 128), BF16),
            pltpu.VMEM((CHIPS, 16, HALF), F32),
            pltpu.VMEM((2, CHIPS, 16, HALF), BF16),
            pltpu.VMEM((2, CHIPS, 16, HALF), BF16),
            pltpu.VMEM((2, SIDE, SIDE, 16, HALF), BF16),
            pltpu.VMEM((2, 2, 3, SIDE, 16, PART), BF16),
            pltpu.VMEM((2, 2, SIDE, 16, PART), BF16),
            pltpu.VMEM((2, 2, 3, 16, PART), BF16),
            dma((2, 13)),
            dma((2, 13)),
            pltpu.VMEM((2, SLOT, HALF), F32),
            pltpu.VMEM((2, SLOT, HALF), F32),
            pltpu.VMEM((16, HALF), F32),
            pltpu.VMEM((16, 128), F32),
            pltpu.VMEM((16, 128), F32),
            pltpu.VMEM((2, SIDE, SIDE, 16, HALF), BF16),
            dma((13,)),
            dma((13,)),
            pltpu.VMEM((2, SLOT, HALF), F32),
            pltpu.VMEM((SLOT, HALF), F32),
            dma((3,)),
            dma((3,)),
        ],
        compiler_params=pltpu.CompilerParams(
            collective_id=0, has_side_effects=True, vmem_limit_bytes=60 * 2**20
        ),
        cost_estimate=pl.CostEstimate(
            flops=3_600_000_000, bytes_accessed=15_000_000, transcendentals=500_000
        ),
    )(
        lengths,
        occupied,
        jnp.swapaxes(queries, 1, 2),
        jnp.swapaxes(latent_cache, 1, 2),
        w_uv,
        w_out,
        w_gate.T,
        w_up.T,
        w_down,
        residual,
        norm_gain.reshape(1, D),
    )


def solution(mesh):
    in_specs = (
        P(("rep", "wide"), None, None),
        P(("rep", "wide"), None, None),
        P(("rep", "wide")),
        P(("rep", "wide")),
        P(("rep", "wide"), None),
        P("wide", None, None),
        P("wide", None),
        P(),
        P(None, "wide"),
        P(None, "wide"),
        P("wide", None),
    )
    out_specs = P(("rep", "wide"), None)
    return jax.shard_map(shards, mesh=mesh, in_specs=in_specs, out_specs=out_specs, check_vma=False)
```

time: 290 us -> 81.3 us (0.28)
  waiting for transfers between devices: 223 us -> 0 us
  Pallas kernels: 0 us -> 78.3 us
  blocking collectives: 25.8 us -> 0 us
  matrix products: 21.4 us -> 0 us
  between operations: 13.2 us -> 0.01 us
  other arithmetic: 4.83 us -> 0 us
    reduce_scatter x2 -> x0, waiting for transfers between devices: 172 us -> none  [the longest x1 86.1 us: shards(): lax.psum_scatter(jnp.dot(picked, w_down, preferred_element_type=jnp.float...]
    pallas_call x0 -> x1, Pallas kernels: none -> 78.3 us  [shards(): pl.pallas_call(layer_kernel, out_shape=jax.ShapeDtypeStruct((SLOT, D), BF...]
    all_gather x1 -> x0, waiting for transfers between devices: 51.1 us -> none  [shards(): lax.all_gather(normed, 'wide', axis=0, tiled=True)]
    all_to_all x1 -> x0, blocking collectives: 25.8 us -> none  [shards(): lax.all_to_all(latent_out, 'wide', split_axis=1, concat_axis=0, tiled=True)]
    dot_general x5 -> x0, matrix products: 16.6 us -> none  [the longest x1 6.84 us: shards(): jnp.dot(picked, w_down, preferred_element_type=jnp.float32)]
    sub x1 -> x0, matrix products: 4.8 us -> none  [shards(): weights = jnp.where(live, jnp.exp(scores - peak), jnp.float32(0.0))]
    convert_element_type x4 -> x0, other arithmetic: 3.05 us -> none  [the longest x1 1.53 us: shards(): return (hidden.astype(jnp.float32) + ffn).astype(jnp.bfloat16)]
  transfers between devices with their start and end apart: 3 -> 0, of which waited for: 3 -> 0; matrix products, arithmetic and copies ran while one was open for 0% -> 0% of each run, Pallas kernels for 0% -> 0%
where the time goes in v1:
time: 81.3 us; the launch traced here: 81 us
  Pallas kernels  78.3 us (96%)
  local copies, waits for them, and re-layouts  2.75 us (3%)
    pallas_call x1, Pallas kernels, shards(): pl.pallas_call(layer_kernel, out_shape=jax.ShapeDtypeStruct((SLOT, D), BF...  78.3 us

profile of v1, /device:TPU:1, one launch (start us, length us, event | category | flops | bytes accessed | tf_op | source)
XLA Modules:
  0.0 81.0 jit_solution(16420354630317903049)
XLA Ops:
  0.0 1.3 %reshape.3.gain = bf16[1,3584]{1,0:T(2,128)(2,1)} reshape(bf16[3584]{0:T(1024)(128)(2,1)} %param.18) | data formatting | bytes 14336 | tf_op jit(solution)/shard_map/reshape | solution.py:430
  1.3 78.3 %shard_map.109 = bf16[8,3584]{1,0:T(8,128)(2,1)} custom-call(s32[8]{0:T(128)} %lengths.1, s32[8]{0:T(128)} %occupied.1, bf16[8,576,128]{2,1,0:T(8,128)(2,1)} %bitcast.7, bf16[8,576,384]{2,1,0:T(8,128)(2,1)} %bitcast.4, bf16[4,512,128]{2,1,0:T(8,128)(2,1)} %w_uv.1, bf16[512,3584]{1,0:T(8,128)(2,1)} %w_out.1, bf16[288,3584]{1,0:T(8,128)(2,1)} %bitcast.5, ...), custom_call_target="tpu_custom_call" | custom-call | flops 3600000000 | bytes 15000000 | tf_op jit(solution)/shard_map/pallas_call | solution.py:371
  79.6 1.4 %copy.13 = bf16[8,3584]{1,0:T(8,128)(2,1)} copy(bf16[8,3584]{1,0:T(8,128)(2,1)} %shard_map.109) | data formatting | bytes 114688

commit v2 on v0

v2 whole, which is shorter than its diff:
```python
import jax
import jax.numpy as jnp
from jax import lax
from jax.experimental import pallas as pl
from jax.experimental.pallas import tpu as pltpu
from jax.sharding import PartitionSpec as P

MESH = pl.DeviceIdType.MESH
F32 = jnp.float32
BF16 = jnp.bfloat16
softmax_scale = 192.0 ** (-0.5)

SIDE = 4
CHIPS = SIDE * SIDE
DEVICES = 2 * CHIPS
SLOT = 8
WAVE = SLOT // 2
HEADS = 128
OWN_HEADS = HEADS // DEVICES
LAT = 512
LANES = LAT // 128
KEY = 576
LMAX = 384
D = 3584
HALF = D // 2
PART = HALF // 2
ROWS = DEVICES * WAVE
FFS = 288
NT = (((1,), (1,)), ((), ()))
TN = (((0,), (0,)), ((), ()))


def hops(offset):
    return sum(min(step, SIDE - step) for step in offset[:2])


OFFSETS = sorted(
    [(dy, dx, dc) for dy in range(SIDE) for dx in range(SIDE) for dc in range(2)][1:],
    key=lambda offset: -hops(offset),
)


def remote(src, dst, send, recv, to):
    return pltpu.make_async_remote_copy(
        src_ref=src,
        dst_ref=dst,
        send_sem=send,
        recv_sem=recv,
        device_id={"wide": to},
        device_id_type=MESH,
    )


def layer_kernel(
    lengths_hbm,
    occupied_hbm,
    queries,
    cache,
    w_uv,
    w_out,
    w_gate,
    w_up,
    w_down,
    residual_hbm,
    gain_hbm,
    out,
    lengths,
    occupied,
    residual,
    gain,
    gain_rows,
    scaled,
    q_v,
    c_v,
    uv_v,
    wo_v,
    gu_v,
    wd_v,
    load_sem,
    attn,
    a2a_out,
    a2a_in,
    a2a_send,
    a2a_recv,
    rowvals,
    values,
    acc,
    p0,
    r0,
    s0,
    r1,
    s1,
    r2,
    mine,
    rs_send,
    rs_recv,
    res_own,
    res_both,
    hid,
    sq_own,
    sq_in,
    gathered,
    ag_send,
    ag_recv,
    swap_send,
    swap_recv,
    up_own,
    acts,
    ends,
    last_own,
    last_in,
    pair_send,
    pair_recv,
):
    me = lax.axis_index("wide")
    core = lax.rem(me, 2)
    chip = me // 2
    x = lax.rem(chip, SIDE)
    y = chip // SIDE
    partner = me + 1 - 2 * core

    def at(cy, cx):
        return (cy * SIDE + cx) * 2 + core

    def along_x(k):
        return lax.rem(x + k, SIDE)

    def along_y(k):
        return lax.rem(y + k, SIDE)

    loads = []

    def load(src, dst):
        copy = pltpu.make_async_copy(src, dst, load_sem.at[len(loads)])
        copy.start()
        loads.append(copy)
        return copy

    count_loads = [load(lengths_hbm, lengths), load(occupied_hbm, occupied)]
    slot_loads = []
    for s in range(SLOT):
        slot_loads.append((load(queries.at[s], q_v.at[s]), load(cache.at[s], c_v.at[s])))

    barrier = pltpu.get_barrier_semaphore()

    def greet(k, carry):
        pl.semaphore_signal(
            barrier, inc=1, device_id={"wide": lax.rem(me + k, DEVICES)}, device_id_type=MESH
        )
        return carry

    lax.fori_loop(1, DEVICES, greet, 0)
    row_loads = [load(residual_hbm, residual), load(gain_hbm, gain)]
    uv_loads = [load(w_uv.at[h], uv_v.at[:, pl.ds(h * 128, 128)]) for h in range(OWN_HEADS)]
    wo_loads = [load(w_out.at[:, pl.ds(j * HALF, HALF)], wo_v.at[j]) for j in range(2)]
    gu_loads = [
        load(w_gate, gu_v.at[pl.ds(0, FFS)]),
        load(w_up, gu_v.at[pl.ds(FFS, FFS)]),
    ]
    wd_loads = [load(w_down.at[:, pl.ds(j * HALF, HALF)], wd_v.at[j]) for j in range(2)]

    def lanes(part):
        return pl.ds(part * PART, PART)

    def upper(rows):
        return lax.broadcasted_iota(jnp.int32, rows.shape, 0) < WAVE

    def stack(rows, more):
        return jnp.where(upper(rows), rows, pltpu.roll(more, WAVE, 0))

    def stack_last(rows, more):
        return jnp.where(upper(rows), pltpu.roll(rows, WAVE, 0), more)

    position = lax.broadcasted_iota(jnp.int32, (HEADS, LMAX), 1)

    def attend(w):
        for i in range(WAVE):
            s = w * WAVE + i
            for copy in slot_loads[s]:
                copy.wait()
            keys = c_v[s]
            scores = lax.dot_general(q_v[s], keys, TN, preferred_element_type=F32)
            scores = jnp.where(position < lengths[s], scores, F32(-1e30))
            peak = jnp.max(scores, axis=1, keepdims=True)
            weights = jnp.exp((scores - peak) * F32(softmax_scale))
            flag = occupied[s].astype(F32)
            probs = (weights * (flag / jnp.sum(weights, axis=1, keepdims=True))).astype(BF16)
            result = lax.dot_general(probs, keys[:LAT], NT, preferred_element_type=F32)
            for lane in range(LANES):
                attn[lane, i] = result[:, lane * 128 : (lane + 1) * 128]

        def pack(t, carry):
            for lane in range(LANES):
                tile = [attn[lane, i, pl.ds(pl.multiple_of(8 * t, 8), 8)] for i in range(WAVE)]
                for odd, join in enumerate((stack, stack_last)):
                    rows = jnp.concatenate([join(tile[0], tile[1]), join(tile[2], tile[3])], axis=0)
                    a2a_out[w, 2 * t + odd, :, lane * 128 : (lane + 1) * 128] = rows.astype(BF16)
            return carry

        lax.fori_loop(0, DEVICES // 2, pack, 0)

    def exchange(w):
        copies = []
        for k, (dy, dx, dc) in enumerate(OFFSETS):
            to = (along_y(dy) * SIDE + along_x(dx)) * 2 + lax.rem(core + dc, 2)
            copies.append(
                remote(
                    a2a_out.at[w, to],
                    a2a_in.at[w, me],
                    a2a_send.at[w, k],
                    a2a_recv.at[w, k],
                    to,
                )
            )
            copies[-1].start()
        a2a_in[w, me] = a2a_out[w, me]
        return copies

    def project(w, copies):
        for copy in copies:
            copy.wait()
        product = jnp.dot(
            a2a_in[w].reshape(DEVICES * OWN_HEADS * WAVE, LAT),
            uv_v[...],
            preferred_element_type=F32,
        )
        for h in range(OWN_HEADS):
            rowvals[h] = product[:, h * 128 : (h + 1) * 128]
        for h in range(OWN_HEADS):
            values[w, :, h * 128 : (h + 1) * 128] = rowvals[
                h, pl.ds(h, ROWS, stride=OWN_HEADS), :
            ].astype(BF16)

    def sum_pair(n, w, product):
        m = 2 * n + w
        p0[m] = product(1 - core).reshape(CHIPS, 8, HALF).astype(BF16)
        copy = remote(p0.at[m], r0.at[m], rs_send.at[m, 0], rs_recv.at[m, 0], partner)
        copy.start()
        acc[w] = product(core).reshape(SIDE, SIDE, 8, HALF)
        return [copy]

    def sum_first(n, w, copies):
        m = 2 * n + w
        for copy in copies:
            copy.wait()
        copies = []

        def place(part, k, i):
            return (i, along_x(k)) if part == 0 else (along_y(k), i)

        def added(part, k, i):
            cy, cx = place(part, k, i)
            block = (cy, cx, slice(None), slice(part * PART, (part + 1) * PART))
            return block, acc[(w, *block)] + r0[m, cy * SIDE + cx, :, block[3]].astype(F32)

        for k in (2, 1, 3):
            for part in range(2):
                for i in range(SIDE):
                    block, total = added(part, k, i)
                    s0[(m, *block)] = total.astype(BF16)
                copies.append(
                    remote(
                        s0.at[m, :, along_x(k), :, lanes(0)]
                        if part == 0
                        else s0.at[m, along_y(k), :, :, lanes(1)],
                        r1.at[m, part, k - 1],
                        rs_send.at[m, 3 * part + k],
                        rs_recv.at[m, 3 * part + k],
                        at(y, along_x(k)) if part == 0 else at(along_y(k), x),
                    )
                )
                copies[-1].start()
        for part in range(2):
            for i in range(SIDE):
                block, total = added(part, 0, i)
                acc[(w, *block)] = total
        return copies

    def sum_second(n, w, copies):
        m = 2 * n + w
        later = []
        for part in range(2):
            for copy in copies[part::2]:
                copy.wait()
            for k in (2, 1, 3, 0):
                to = along_y(k) if part == 0 else along_x(k)
                if part == 0:
                    total = acc[w, to, x, :, :PART]
                else:
                    total = acc[w, y, to, :, PART:]
                for i in range(3):
                    total += r1[m, part, i, to].astype(F32)
                if k == 0:
                    mine[w, :, part * PART : (part + 1) * PART] = total
                else:
                    s1[m, part, to] = total.astype(BF16)
                    later.append(
                        remote(
                            s1.at[m, part, to],
                            r2.at[m, part, k - 1],
                            rs_send.at[m, 6 + 3 * part + k],
                            rs_recv.at[m, 6 + 3 * part + k],
                            at(to, x) if part == 0 else at(y, to),
                        )
                    )
                    later[-1].start()
        return later

    def sum_last(n, w, copies):
        m = 2 * n + w
        for copy in copies:
            copy.wait()
        sums = []
        for part in range(2):
            total = mine[w, :, part * PART : (part + 1) * PART]
            for i in range(3):
                total += r2[m, part, i].astype(F32)
            sums.append(total)
        return sums

    def hide(w, copies):
        sums = sum_last(0, w, copies)
        if w == 0:
            res_copy.wait()
        square = jnp.zeros((8, 1), F32)
        for part in range(2):
            columns = slice(part * PART, (part + 1) * PART)
            join = stack if w == 0 else stack_last
            rows = join(res_both[0, :, columns], res_both[1, :, columns]) + sums[part]
            rows = rows.astype(BF16).astype(F32)
            hid[w, :, columns] = rows
            square += jnp.sum(rows * rows, axis=1, keepdims=True)
        sq_own[w] = jnp.broadcast_to(square, (8, 128))
        copy = remote(
            sq_own.at[w], sq_in.at[w], pair_send.at[1 + w], pair_recv.at[1 + w], partner
        )
        copy.start()
        return [copy]

    def gather_first(w, copies):
        copies[0].wait()
        inverse = lax.rsqrt((sq_own[w, :, :1] + sq_in[w, :, :1]) * F32(1.0 / D) + F32(1e-6))
        gathered[w, core, y, x] = (hid[w] * inverse * scaled[...]).astype(BF16)
        copies = []
        for k in (2, 1, 3):
            for part, to in ((0, at(along_y(k), x)), (1, at(y, along_x(k)))):
                place = gathered.at[w, core, y, x, :, lanes(part)]
                copies.append(
                    remote(
                        place,
                        place,
                        ag_send.at[w, 3 * part + k],
                        ag_recv.at[w, 3 * part + k],
                        to,
                    )
                )
                copies[-1].start()
        return copies

    def column(w, part, k):
        if part == 0:
            return gathered.at[w, core, :, along_x(k), :, lanes(0)]
        return gathered.at[w, core, along_y(k), :, :, lanes(1)]

    def swap(w, part, k):
        place = column(w, part, k)
        copy = remote(
            place, place, swap_send.at[w, part, k], swap_recv.at[w, part, k], partner
        )
        copy.start()
        return copy

    def gather_second(w, copies):
        for copy in copies:
            copy.wait()
        copies = []
        for k in (2, 1, 3):
            for part, to in ((0, at(y, along_x(k))), (1, at(along_y(k), x))):
                place = column(w, part, 0)
                copies.append(
                    remote(
                        place,
                        place,
                        ag_send.at[w, 6 + 3 * part + k],
                        ag_recv.at[w, 6 + 3 * part + k],
                        to,
                    )
                )
                copies[-1].start()
        return copies, [swap(w, 0, 0), swap(w, 1, 0)]

    def forward(w, state):
        copies, swaps = state
        for i, k in ((2, 1), (4, 3), (0, 2)):
            for part in range(2):
                copies[i + part].wait()
                swaps.append(swap(w, part, SIDE - k))
        return swaps

    def wide(w, j):
        rows = gathered[w, j].astype(F32).reshape(ROWS, HALF).astype(BF16)
        return lax.dot_general(
            gu_v[:, pl.ds(pl.multiple_of(j * HALF, 128), HALF)],
            rows,
            NT,
            preferred_element_type=F32,
        )

    def expand_own(w):
        up_own[w] = wide(w, core)

    def expand(w, swaps):
        for copy in swaps:
            copy.wait()
        up = up_own[w] + wide(w, 1 - core)
        gate = up[:FFS]
        acts[w] = (gate / (1.0 + jnp.exp(-gate)) * up[FFS:]).astype(BF16)

    def inward(w):
        return lambda j: lax.dot_general(acts[w], wd_v[j], TN, preferred_element_type=F32)

    def finish(w, copies):
        sums = sum_last(1, w, copies)
        for part in range(2):
            columns = slice(part * PART, (part + 1) * PART)
            ends[w, :, columns] = hid[w, :, columns] + sums[part]

    for copy in count_loads:
        copy.wait()
    attend(0)
    pl.semaphore_wait(barrier, DEVICES - 1)
    sent0 = exchange(0)
    for copy in row_loads:
        copy.wait()
    for j in range(2):
        res_own[j] = residual[:, j * HALF : (j + 1) * HALF].astype(F32)
    res_copy = remote(
        res_own.at[1 - core], res_both.at[core], pair_send.at[0], pair_recv.at[0], partner
    )
    res_copy.start()
    res_both[core] = res_own[core]
    attend(1)
    sent1 = exchange(1)
    gain_rows[...] = gain[...].astype(F32)
    for t in range(HALF // 128):
        row = gain_rows[pl.ds(core * (HALF // 128) + t, 1), :]
        scaled[:, t * 128 : (t + 1) * 128] = jnp.broadcast_to(row, (8, 128))
    for copy in uv_loads + wo_loads:
        copy.wait()

    def outward(w):
        return lambda j: jnp.dot(values[w], wo_v[j], preferred_element_type=F32)

    project(0, sent0)
    step0 = sum_pair(0, 0, outward(0))
    step0 = sum_first(0, 0, step0)
    project(1, sent1)
    step1 = sum_pair(0, 1, outward(1))
    step0 = sum_second(0, 0, step0)
    step1 = sum_first(0, 1, step1)
    step0 = hide(0, step0)
    step0 = gather_first(0, step0)
    step1 = sum_second(0, 1, step1)
    step0 = gather_second(0, step0)
    for copy in gu_loads + wd_loads:
        copy.wait()
    step1 = hide(1, step1)
    step1 = gather_first(1, step1)
    step0 = forward(0, step0)
    expand_own(0)
    step1 = gather_second(1, step1)
    expand(0, step0)
    step0 = sum_pair(1, 0, inward(0))
    step0 = sum_first(1, 0, step0)
    step1 = forward(1, step1)
    expand_own(1)
    expand(1, step1)
    step1 = sum_pair(1, 1, inward(1))
    step0 = sum_second(1, 0, step0)
    step1 = sum_first(1, 1, step1)
    finish(0, step0)
    step1 = sum_second(1, 1, step1)
    finish(1, step1)
    last_own[0] = stack(ends[0], ends[1])
    last_own[1] = stack_last(ends[0], ends[1])
    last = remote(last_own.at[1 - core], last_in, pair_send.at[3], pair_recv.at[3], partner)
    last.start()
    last.wait()
    out[:, pl.ds(pl.multiple_of(core * HALF, 128), HALF)] = last_own[core].astype(BF16)
    out[:, pl.ds(pl.multiple_of((1 - core) * HALF, 128), HALF)] = last_in[...].astype(BF16)


def shards(
    queries, latent_cache, lengths, occupied, residual, w_uv, w_out, norm_gain, w_gate, w_up, w_down
):
    hbm = pl.BlockSpec(memory_space=pl.ANY)
    vmem = pl.BlockSpec(memory_space=pltpu.VMEM)
    dma = pltpu.SemaphoreType.DMA
    return pl.pallas_call(
        layer_kernel,
        out_shape=jax.ShapeDtypeStruct((SLOT, D), BF16),
        in_specs=[hbm] * 11,
        out_specs=vmem,
        scratch_shapes=[
            pltpu.SMEM((SLOT,), jnp.int32),
            pltpu.SMEM((SLOT,), jnp.int32),
            pltpu.VMEM((SLOT, D), BF16),
            pltpu.VMEM((D // 128, 128), BF16),
            pltpu.VMEM((D // 128, 128), F32),
            pltpu.VMEM((8, HALF), F32),
            pltpu.VMEM((SLOT, KEY, HEADS), BF16),
            pltpu.VMEM((SLOT, KEY, LMAX), BF16),
            pltpu.VMEM((LAT, OWN_HEADS * 128), BF16),
            pltpu.VMEM((2, OWN_HEADS * 128, HALF), BF16),
            pltpu.VMEM((2 * FFS, D), BF16),
            pltpu.VMEM((2, FFS, HALF), BF16),
            dma((2 * SLOT + OWN_HEADS + 10,)),
            pltpu.VMEM((LANES, WAVE, HEADS, 128), F32),
            pltpu.VMEM((2, DEVICES, OWN_HEADS * WAVE, LAT), BF16),
            pltpu.VMEM((2, DEVICES, OWN_HEADS * WAVE, LAT), BF16),
            dma((2, DEVICES)),
            dma((2, DEVICES)),
            pltpu.VMEM((OWN_HEADS, ROWS * OWN_HEADS, 128), F32),
            pltpu.VMEM((2, ROWS, OWN_HEADS * 128), BF16),
            pltpu.VMEM((2, SIDE, SIDE, 8, HALF), F32),
            pltpu.VMEM((4, CHIPS, 8, HALF), BF16),
            pltpu.VMEM((4, CHIPS, 8, HALF), BF16),
            pltpu.VMEM((4, SIDE, SIDE, 8, HALF), BF16),
            pltpu.VMEM((4, 2, 3, SIDE, 8, PART), BF16),
            pltpu.VMEM((4, 2, SIDE, 8, PART), BF16),
            pltpu.VMEM((4, 2, 3, 8, PART), BF16),
            pltpu.VMEM((2, 8, HALF), F32),
            dma((4, 13)),
            dma((4, 13)),
            pltpu.VMEM((2, SLOT, HALF), F32),
            pltpu.VMEM((2, SLOT, HALF), F32),
            pltpu.VMEM((2, 8, HALF), F32),
            pltpu.VMEM((2, 8, 128), F32),
            pltpu.VMEM((2, 8, 128), F32),
            pltpu.VMEM((2, 2, SIDE, SIDE, 8, HALF), BF16),
            dma((2, 13)),
            dma((2, 13)),
            dma((2, 2, SIDE)),
            dma((2, 2, SIDE)),
            pltpu.VMEM((2, 2 * FFS, ROWS), F32),
            pltpu.VMEM((2, FFS, ROWS), BF16),
            pltpu.VMEM((2, 8, HALF), F32),
            pltpu.VMEM((2, SLOT, HALF), F32),
            pltpu.VMEM((SLOT, HALF), F32),
            dma((4,)),
            dma((4,)),
        ],
        compiler_params=pltpu.CompilerParams(
            collective_id=0, has_side_effects=True, vmem_limit_bytes=60 * 2**20
        ),
        cost_estimate=pl.CostEstimate(
            flops=3_600_000_000, bytes_accessed=15_000_000, transcendentals=500_000
        ),
    )(
        lengths,
        occupied,
        jnp.swapaxes(queries, 1, 2),
        jnp.swapaxes(latent_cache, 1, 2),
        w_uv,
        w_out,
        w_gate.T,
        w_up.T,
        w_down,
        residual,
        norm_gain.reshape(D // 128, 128),
    )


def solution(mesh):
    in_specs = (
        P(("rep", "wide"), None, None),
        P(("rep", "wide"), None, None),
        P(("rep", "wide")),
        P(("rep", "wide")),
        P(("rep", "wide"), None),
        P("wide", None, None),
        P("wide", None),
        P(),
        P(None, "wide"),
        P(None, "wide"),
        P("wide", None),
    )
    out_specs = P(("rep", "wide"), None)
    return jax.shard_map(shards, mesh=mesh, in_specs=in_specs, out_specs=out_specs, check_vma=False)
```

time: 290 us -> 66.3 us (0.23)
  waiting for transfers between devices: 223 us -> 0 us
  Pallas kernels: 0 us -> 64.8 us
  blocking collectives: 25.8 us -> 0 us
  matrix products: 21.4 us -> 0 us
  between operations: 13.2 us -> 0.01 us
  other arithmetic: 4.83 us -> 0 us
    reduce_scatter x2 -> x0, waiting for transfers between devices: 172 us -> none  [the longest x1 86.1 us: shards(): lax.psum_scatter(jnp.dot(picked, w_down, preferred_element_type=jnp.float...]
    pallas_call x0 -> x1, Pallas kernels: none -> 64.8 us  [shards(): pl.pallas_call(layer_kernel, out_shape=jax.ShapeDtypeStruct((SLOT, D), BF...]
    all_gather x1 -> x0, waiting for transfers between devices: 51.1 us -> none  [shards(): lax.all_gather(normed, 'wide', axis=0, tiled=True)]
    all_to_all x1 -> x0, blocking collectives: 25.8 us -> none  [shards(): lax.all_to_all(latent_out, 'wide', split_axis=1, concat_axis=0, tiled=True)]
    dot_general x5 -> x0, matrix products: 16.6 us -> none  [the longest x1 6.84 us: shards(): jnp.dot(picked, w_down, preferred_element_type=jnp.float32)]
    sub x1 -> x0, matrix products: 4.8 us -> none  [shards(): weights = jnp.where(live, jnp.exp(scores - peak), jnp.float32(0.0))]
    convert_element_type x4 -> x0, other arithmetic: 3.05 us -> none  [the longest x1 1.53 us: shards(): return (hidden.astype(jnp.float32) + ffn).astype(jnp.bfloat16)]
  transfers between devices with their start and end apart: 3 -> 0, of which waited for: 3 -> 0; matrix products, arithmetic and copies ran while one was open for 0% -> 0% of each run, Pallas kernels for 0% -> 0%
where the time goes in v2:
time: 66.3 us; the launch traced here: 66.2 us
  Pallas kernels  64.8 us (98%)
  local copies, waits for them, and re-layouts  1.45 us (2%)
    pallas_call x1, Pallas kernels, shards(): pl.pallas_call(layer_kernel, out_shape=jax.ShapeDtypeStruct((SLOT, D), BF...  64.8 us
    unnamed x1, local copies, waits for them, and re-layouts  1.45 us

profile of v2, /device:TPU:1, one launch (start us, length us, event | category | flops | bytes accessed | tf_op | source)
XLA Modules:
  0.0 66.2 jit_solution(5490842002567658463)
XLA Ops:
  0.0 64.8 %shard_map.109 = bf16[8,3584]{1,0:T(8,128)(2,1)} custom-call(s32[8]{0:T(128)} %lengths_hbm.1, s32[8]{0:T(128)} %occupied_hbm.1, bf16[8,576,128]{2,1,0:T(8,128)(2,1)} %bitcast.8, bf16[8,576,384]{2,1,0:T(8,128)(2,1)} %bitcast.5, bf16[4,512,128]{2,1,0:T(8,128)(2,1)} %w_uv.1, bf16[512,3584]{1,0:T(8,128)(2,1)} %w_out.1, bf16[288,3584]{1,0:T(8,128)(2,1)} %bitcast.6, ...), custom_call_target="tpu_custom_call" | custom-call | flops 3600000000 | bytes 15000000 | tf_op jit(solution)/shard_map/pallas_call | solution.py:499
  64.8 1.4 %copy.13 = bf16[8,3584]{1,0:T(8,128)(2,1)} copy(bf16[8,3584]{1,0:T(8,128)(2,1)} %shard_map.109) | data formatting | bytes 114688

commit v3 on v2

v3 whole, which is shorter than its diff:
```python
import jax
import jax.numpy as jnp
from jax import lax
from jax.experimental import pallas as pl
from jax.experimental.pallas import tpu as pltpu
from jax.sharding import PartitionSpec as P

MESH = pl.DeviceIdType.MESH
F32 = jnp.float32
BF16 = jnp.bfloat16
softmax_scale = 192.0 ** (-0.5)

SIDE = 4
CHIPS = SIDE * SIDE
DEVICES = 2 * CHIPS
SLOT = 8
WAVE = SLOT // 2
HEADS = 128
OWN_HEADS = HEADS // DEVICES
LAT = 512
LANES = LAT // 128
KEY = 576
LMAX = 384
D = 3584
HALF = D // 2
ROWS = DEVICES * WAVE
FFS = 288
NT = (((1,), (1,)), ((), ()))
TN = (((0,), (0,)), ((), ()))


def hops(offset):
    return sum(min(step, SIDE - step) for step in offset[:2])


CHIP_OFFSETS = sorted(
    [(dy, dx) for dy in range(SIDE) for dx in range(SIDE)][1:], key=lambda offset: -hops(offset)
)

OFFSETS = sorted(
    [(dy, dx, dc) for dy in range(SIDE) for dx in range(SIDE) for dc in range(2)][1:],
    key=lambda offset: -hops(offset),
)


def wait_bytes(ref, sem):
    pltpu.make_async_copy(ref, ref, sem).wait()


def remote(src, dst, send, recv, to):
    return pltpu.make_async_remote_copy(
        src_ref=src,
        dst_ref=dst,
        send_sem=send,
        recv_sem=recv,
        device_id={"wide": to},
        device_id_type=MESH,
    )


def layer_kernel(
    lengths_hbm,
    occupied_hbm,
    queries,
    cache,
    w_uv,
    w_out,
    w_gate,
    w_up,
    w_down,
    residual_hbm,
    gain_hbm,
    out,
    lengths,
    occupied,
    residual,
    gain,
    gain_rows,
    scaled,
    q_v,
    c_v,
    uv_v,
    wo_v,
    gu_v,
    wd_v,
    load_sem,
    attn,
    a2a_out,
    a2a_in,
    a2a_send,
    a2a_recv,
    rowvals,
    values,
    acc,
    s0,
    rd,
    pair_of_send,
    pair_of_recv,
    rd_send,
    rd_recv,
    res_own,
    res_both,
    hid,
    sq_own,
    sq_in,
    gathered,
    ag_send,
    ag_recv,
    swap_send,
    swap_recv,
    up_own,
    acts,
    ends,
    last_own,
    last_in,
    pair_send,
    pair_recv,
):
    me = lax.axis_index("wide")
    core = lax.rem(me, 2)
    chip = me // 2
    x = lax.rem(chip, SIDE)
    y = chip // SIDE
    partner = me + 1 - 2 * core

    def at(cy, cx):
        return (cy * SIDE + cx) * 2 + core

    def along_x(k):
        return lax.rem(x + k, SIDE)

    def along_y(k):
        return lax.rem(y + k, SIDE)

    loads = []

    def load(src, dst, same=0):
        copy = pltpu.make_async_copy(src, dst, load_sem.at[len(loads) - same])
        copy.start()
        if not same:
            loads.append(copy)
        return copy

    count_loads = [load(lengths_hbm, lengths), load(occupied_hbm, occupied)]
    query_loads = []
    cache_loads = []
    for w in range(2):
        wave = pl.ds(w * WAVE, WAVE)
        query_loads.append(load(queries.at[wave], q_v.at[wave]))
        if w == 0:
            cache_loads += [load(cache.at[s], c_v.at[s]) for s in range(WAVE)]
        else:
            cache_loads.append(load(cache.at[wave], c_v.at[wave]))

    barrier = pltpu.get_barrier_semaphore()

    def greet(k, carry):
        pl.semaphore_signal(
            barrier, inc=1, device_id={"wide": lax.rem(me + k, DEVICES)}, device_id_type=MESH
        )
        return carry

    lax.fori_loop(1, DEVICES, greet, 0)
    row_loads = [load(residual_hbm, residual), load(gain_hbm, gain)]
    for h in range(OWN_HEADS):
        load(w_uv.at[h], uv_v.at[:, pl.ds(h * 128, 128)], same=min(h, 1))
    uv_sem = load_sem.at[len(loads) - 1]
    own_half = pl.ds(pl.multiple_of(core * HALF, 128), HALF)
    wo_loads = [load(w_out.at[:, own_half], wo_v.at[core])]
    load(w_gate, gu_v.at[pl.ds(0, FFS)])
    load(w_up, gu_v.at[pl.ds(FFS, FFS)], same=1)
    gu_sem = load_sem.at[len(loads) - 1]
    wd_loads = [load(w_down.at[:, own_half], wd_v.at[core])]

    def upper(rows):
        return lax.broadcasted_iota(jnp.int32, rows.shape, 0) < WAVE

    def stack(rows, more):
        return jnp.where(upper(rows), rows, pltpu.roll(more, WAVE, 0))

    def stack_last(rows, more):
        return jnp.where(upper(rows), pltpu.roll(rows, WAVE, 0), more)

    position = lax.broadcasted_iota(jnp.int32, (HEADS, LMAX), 1)

    def attend(w):
        for i in range(WAVE):
            s = w * WAVE + i
            if i == 0:
                query_loads[w].wait()
            if s <= WAVE:
                cache_loads[s].wait()
            keys = c_v[s]
            scores = lax.dot_general(q_v[s], keys, TN, preferred_element_type=F32)
            scores = jnp.where(position < lengths[s], scores, F32(-1e30))
            peak = jnp.max(scores, axis=1, keepdims=True)
            weights = jnp.exp((scores - peak) * F32(softmax_scale))
            flag = occupied[s].astype(F32)
            probs = (weights * (flag / jnp.sum(weights, axis=1, keepdims=True))).astype(BF16)
            result = lax.dot_general(probs, keys[:LAT], NT, preferred_element_type=F32)
            for lane in range(LANES):
                attn[lane, i] = result[:, lane * 128 : (lane + 1) * 128]

        def pack(t, carry):
            for lane in range(LANES):
                tile = [attn[lane, i, pl.ds(pl.multiple_of(8 * t, 8), 8)] for i in range(WAVE)]
                for odd, join in enumerate((stack, stack_last)):
                    rows = jnp.concatenate([join(tile[0], tile[1]), join(tile[2], tile[3])], axis=0)
                    a2a_out[w, 2 * t + odd, :, lane * 128 : (lane + 1) * 128] = rows.astype(BF16)
            return carry

        lax.fori_loop(0, DEVICES // 2, pack, 0)

    def exchange(w):
        for dy, dx, dc in OFFSETS:
            to = (along_y(dy) * SIDE + along_x(dx)) * 2 + lax.rem(core + dc, 2)
            remote(
                a2a_out.at[w, to], a2a_in.at[w, me], a2a_send.at[w], a2a_recv.at[w], to
            ).start()
        a2a_in[w, me] = a2a_out[w, me]

    def project(w):
        others = a2a_in.at[w, pl.ds(0, DEVICES - 1)]
        wait_bytes(others, a2a_recv.at[w])
        wait_bytes(others, a2a_send.at[w])
        product = jnp.dot(
            a2a_in[w].reshape(DEVICES * OWN_HEADS * WAVE, LAT),
            uv_v[...],
            preferred_element_type=F32,
        )
        for h in range(OWN_HEADS):
            rowvals[h] = product[:, h * 128 : (h + 1) * 128]
        for h in range(OWN_HEADS):
            values[w, core, :, h * 128 : (h + 1) * 128] = rowvals[
                h, pl.ds(h, ROWS, stride=OWN_HEADS), :
            ].astype(BF16)

    def sum_pair(n, w, given, product):
        m = 2 * n + w
        place = given.at[w, core]
        copy = remote(place, place, pair_of_send.at[m], pair_of_recv.at[m], partner)
        copy.start()
        acc[w] = product(core).reshape(SIDE, SIDE, 8, HALF)
        copy.wait()
        acc[w] += product(1 - core).reshape(SIDE, SIDE, 8, HALF)

    def sum_start(n, w):
        m = 2 * n + w
        for i, (dy, dx) in enumerate(CHIP_OFFSETS):
            to = (along_y(dy), along_x(dx))
            s0[(m, *to)] = acc[(w, *to)].astype(BF16)
            remote(s0.at[(m, *to)], rd.at[m, i], rd_send.at[m], rd_recv.at[m], at(*to)).start()

    def sum_end(n, w):
        m = 2 * n + w
        wait_bytes(rd.at[m], rd_recv.at[m])
        wait_bytes(rd.at[m], rd_send.at[m])
        total = acc[w, y, x]
        for i in range(CHIPS - 1):
            total += rd[m, i].astype(F32)
        return total

    def hide(w):
        if w == 0:
            res_copy.wait()
        join = stack if w == 0 else stack_last
        rows = join(res_both[0], res_both[1]) + sum_end(0, w)
        rows = rows.astype(BF16).astype(F32)
        hid[w] = rows
        square = jnp.sum(rows * rows, axis=1, keepdims=True)
        sq_own[w] = jnp.broadcast_to(square, (8, 128))
        copy = remote(
            sq_own.at[w], sq_in.at[w], pair_send.at[1 + w], pair_recv.at[1 + w], partner
        )
        copy.start()
        return copy

    def gather(w, copy):
        copy.wait()
        inverse = lax.rsqrt((sq_own[w, :, :1] + sq_in[w, :, :1]) * F32(1.0 / D) + F32(1e-6))
        gathered[w, core, y, x] = (hid[w] * inverse * scaled[...]).astype(BF16)
        place = gathered.at[w, core, y, x]
        for dy, dx in CHIP_OFFSETS:
            to = at(along_y(dy), along_x(dx))
            remote(place, place, ag_send.at[w], ag_recv.at[w, dy], to).start()

    def forward(w):
        for dy in (2, 1, 3, 0):
            row = gathered.at[w, core, along_y((SIDE - dy) % SIDE)]
            wait_bytes(row.at[pl.ds(0, SIDE if dy else SIDE - 1)], ag_recv.at[w, dy])
            remote(row, row, swap_send.at[w], swap_recv.at[w], partner).start()

    def wide(w, j):
        rows = gathered[w, j].astype(F32).reshape(ROWS, HALF).astype(BF16)
        return lax.dot_general(
            gu_v[:, pl.ds(pl.multiple_of(j * HALF, 128), HALF)],
            rows,
            NT,
            preferred_element_type=F32,
        )

    def expand_own(w):
        up_own[w] = wide(w, core)

    def expand(w):
        wait_bytes(gathered.at[w, 1 - core], swap_recv.at[w])
        wait_bytes(gathered.at[w, 1 - core], swap_send.at[w])
        up = up_own[w] + wide(w, 1 - core)
        gate = up[:FFS]
        acts[w, core] = (gate / (1.0 + jnp.exp(-gate)) * up[FFS:]).astype(BF16)

    def inward(w):
        return lambda j: lax.dot_general(acts[w, j], wd_v[j], TN, preferred_element_type=F32)

    def finish(w):
        ends[w] = hid[w] + sum_end(1, w)

    for copy in count_loads:
        copy.wait()
    attend(0)
    pl.semaphore_wait(barrier, DEVICES - 1)
    exchange(0)
    for copy in row_loads:
        copy.wait()
    for j in range(2):
        res_own[j] = residual[:, j * HALF : (j + 1) * HALF].astype(F32)
    res_copy = remote(
        res_own.at[1 - core], res_both.at[core], pair_send.at[0], pair_recv.at[0], partner
    )
    res_copy.start()
    other_half = pl.ds(pl.multiple_of((1 - core) * HALF, 128), HALF)
    wo_copy = remote(
        w_out.at[:, other_half], wo_v.at[core], pair_send.at[4], pair_recv.at[4], partner
    )
    wd_copy = remote(
        w_down.at[:, other_half], wd_v.at[core], pair_send.at[5], pair_recv.at[5], partner
    )
    wo_copy.start()
    wd_copy.start()
    res_both[core] = res_own[core]
    attend(1)
    exchange(1)
    gain_rows[...] = gain[...].astype(F32)
    for t in range(HALF // 128):
        row = gain_rows[pl.ds(core * (HALF // 128) + t, 1), :]
        scaled[:, t * 128 : (t + 1) * 128] = jnp.broadcast_to(row, (8, 128))
    wait_bytes(uv_v, uv_sem)
    wo_loads[0].wait()

    def outward(w):
        return lambda j: jnp.dot(values[w, j], wo_v[j], preferred_element_type=F32)

    project(0)
    wo_copy.wait()
    sum_pair(0, 0, values, outward(0))
    sum_start(0, 0)
    project(1)
    sum_pair(0, 1, values, outward(1))
    sum_start(0, 1)
    square0 = hide(0)
    gather(0, square0)
    wait_bytes(gu_v, gu_sem)
    wd_loads[0].wait()
    wd_copy.wait()
    square1 = hide(1)
    gather(1, square1)
    forward(0)
    expand_own(0)
    expand(0)
    sum_pair(1, 0, acts, inward(0))
    sum_start(1, 0)
    forward(1)
    expand_own(1)
    expand(1)
    sum_pair(1, 1, acts, inward(1))
    sum_start(1, 1)
    finish(0)
    finish(1)
    last_own[0] = stack(ends[0], ends[1])
    last_own[1] = stack_last(ends[0], ends[1])
    last = remote(last_own.at[1 - core], last_in, pair_send.at[3], pair_recv.at[3], partner)
    last.start()
    for w in range(2):
        wait_bytes(gathered.at[w, core, pl.ds(0, SIDE - 1)], ag_send.at[w])
        wait_bytes(gathered.at[w, core, 0, pl.ds(0, SIDE - 1)], ag_send.at[w])
    last.wait()
    out[:, pl.ds(pl.multiple_of(core * HALF, 128), HALF)] = last_own[core].astype(BF16)
    out[:, pl.ds(pl.multiple_of((1 - core) * HALF, 128), HALF)] = last_in[...].astype(BF16)


def shards(
    queries, latent_cache, lengths, occupied, residual, w_uv, w_out, norm_gain, w_gate, w_up, w_down
):
    hbm = pl.BlockSpec(memory_space=pl.ANY)
    vmem = pl.BlockSpec(memory_space=pltpu.VMEM)
    dma = pltpu.SemaphoreType.DMA
    return pl.pallas_call(
        layer_kernel,
        out_shape=jax.ShapeDtypeStruct((SLOT, D), BF16),
        in_specs=[hbm] * 11,
        out_specs=vmem,
        scratch_shapes=[
            pltpu.SMEM((SLOT,), jnp.int32),
            pltpu.SMEM((SLOT,), jnp.int32),
            pltpu.VMEM((SLOT, D), BF16),
            pltpu.VMEM((D // 128, 128), BF16),
            pltpu.VMEM((D // 128, 128), F32),
            pltpu.VMEM((8, HALF), F32),
            pltpu.VMEM((SLOT, KEY, HEADS), BF16),
            pltpu.VMEM((SLOT, KEY, LMAX), BF16),
            pltpu.VMEM((LAT, OWN_HEADS * 128), BF16),
            pltpu.VMEM((2, OWN_HEADS * 128, HALF), BF16),
            pltpu.VMEM((2 * FFS, D), BF16),
            pltpu.VMEM((2, FFS, HALF), BF16),
            dma((15,)),
            pltpu.VMEM((LANES, WAVE, HEADS, 128), F32),
            pltpu.VMEM((2, DEVICES, OWN_HEADS * WAVE, LAT), BF16),
            pltpu.VMEM((2, DEVICES, OWN_HEADS * WAVE, LAT), BF16),
            dma((2,)),
            dma((2,)),
            pltpu.VMEM((OWN_HEADS, ROWS * OWN_HEADS, 128), F32),
            pltpu.VMEM((2, 2, ROWS, OWN_HEADS * 128), BF16),
            pltpu.VMEM((2, SIDE, SIDE, 8, HALF), F32),
            pltpu.VMEM((4, SIDE, SIDE, 8, HALF), BF16),
            pltpu.VMEM((4, CHIPS - 1, 8, HALF), BF16),
            dma((4,)),
            dma((4,)),
            dma((4,)),
            dma((4,)),
            pltpu.VMEM((2, SLOT, HALF), F32),
            pltpu.VMEM((2, SLOT, HALF), F32),
            pltpu.VMEM((2, 8, HALF), F32),
            pltpu.VMEM((2, 8, 128), F32),
            pltpu.VMEM((2, 8, 128), F32),
            pltpu.VMEM((2, 2, SIDE, SIDE, 8, HALF), BF16),
            dma((2,)),
            dma((2, SIDE)),
            dma((2,)),
            dma((2,)),
            pltpu.VMEM((2, 2 * FFS, ROWS), F32),
            pltpu.VMEM((2, 2, FFS, ROWS), BF16),
            pltpu.VMEM((2, 8, HALF), F32),
            pltpu.VMEM((2, SLOT, HALF), F32),
            pltpu.VMEM((SLOT, HALF), F32),
            dma((6,)),
            dma((6,)),
        ],
        compiler_params=pltpu.CompilerParams(
            collective_id=0, has_side_effects=True, vmem_limit_bytes=60 * 2**20
        ),
        cost_estimate=pl.CostEstimate(
            flops=3_600_000_000, bytes_accessed=15_000_000, transcendentals=500_000
        ),
    )(
        lengths,
        occupied,
        jnp.swapaxes(queries, 1, 2),
        jnp.swapaxes(latent_cache, 1, 2),
        w_uv,
        w_out,
        w_gate.T,
        w_up.T,
        w_down,
        residual,
        norm_gain.reshape(D // 128, 128),
    )


def solution(mesh):
    in_specs = (
        P(("rep", "wide"), None, None),
        P(("rep", "wide"), None, None),
        P(("rep", "wide")),
        P(("rep", "wide")),
        P(("rep", "wide"), None),
        P("wide", None, None),
        P("wide", None),
        P(),
        P(None, "wide"),
        P(None, "wide"),
        P("wide", None),
    )
    out_specs = P(("rep", "wide"), None)
    return jax.shard_map(shards, mesh=mesh, in_specs=in_specs, out_specs=out_specs, check_vma=False)
```

time: 66.3 us -> 60.6 us (0.914)
  Pallas kernels: 64.8 us -> 59 us
    pallas_call x1, Pallas kernels: 64.8 us -> 59 us  [shards(): pl.pallas_call(layer_kernel, out_shape=jax.ShapeDtypeStruct((SLOT, D), BF...]
where the time goes in v3:
time: 60.6 us; the launch traced here: 60.5 us
  Pallas kernels  59 us (97%)
  local copies, waits for them, and re-layouts  1.45 us (2%)
    pallas_call x1, Pallas kernels, shards(): pl.pallas_call(layer_kernel, out_shape=jax.ShapeDtypeStruct((SLOT, D), BF...  59 us
    unnamed x1, local copies, waits for them, and re-layouts  1.45 us

profile of v3, /device:TPU:1, one launch (start us, length us, event | category | flops | bytes accessed | tf_op | source)
XLA Modules:
  0.0 60.5 jit_solution(15702766995355212416)
XLA Ops:
  0.0 59.0 %shard_map.109 = bf16[8,3584]{1,0:T(8,128)(2,1)} custom-call(s32[8]{0:T(128)} %lengths_hbm.1, s32[8]{0:T(128)} %occupied_hbm.1, bf16[8,576,128]{2,1,0:T(8,128)(2,1)} %bitcast.8, bf16[8,576,384]{2,1,0:T(8,128)(2,1)} %bitcast.5, bf16[4,512,128]{2,1,0:T(8,128)(2,1)} %w_uv.1, bf16[512,3584]{1,0:T(8,128)(2,1)} %w_out.1, bf16[288,3584]{1,0:T(8,128)(2,1)} %bitcast.6, ...), custom_call_target="tpu_custom_call" | custom-call | flops 3600000000 | bytes 15000000 | tf_op jit(solution)/shard_map/pallas_call | solution.py:397
  59.0 1.4 %copy.13 = bf16[8,3584]{1,0:T(8,128)(2,1)} copy(bf16[8,3584]{1,0:T(8,128)(2,1)} %shard_map.109) | data formatting | bytes 114688

commit v4 on v3

--- a/solution.py
+++ b/solution.py
@@ -144,13 +144,9 @@
     count_loads = [load(lengths_hbm, lengths), load(occupied_hbm, occupied)]
     query_loads = []
     cache_loads = []
-    for w in range(2):
-        wave = pl.ds(w * WAVE, WAVE)
-        query_loads.append(load(queries.at[wave], q_v.at[wave]))
-        if w == 0:
-            cache_loads += [load(cache.at[s], c_v.at[s]) for s in range(WAVE)]
-        else:
-            cache_loads.append(load(cache.at[wave], c_v.at[wave]))
+    for part in [pl.ds(s, 1) for s in range(WAVE)] + [pl.ds(WAVE, WAVE)]:
+        query_loads.append(load(queries.at[part], q_v.at[part]))
+        cache_loads.append(load(cache.at[part], c_v.at[part]))
 
     barrier = pltpu.get_barrier_semaphore()
 
@@ -186,9 +182,8 @@
     def attend(w):
         for i in range(WAVE):
             s = w * WAVE + i
-            if i == 0:
-                query_loads[w].wait()
             if s <= WAVE:
+                query_loads[s].wait()
                 cache_loads[s].wait()
             keys = c_v[s]
             scores = lax.dot_general(q_v[s], keys, TN, preferred_element_type=F32)
@@ -412,7 +407,7 @@
             pltpu.VMEM((2, OWN_HEADS * 128, HALF), BF16),
             pltpu.VMEM((2 * FFS, D), BF16),
             pltpu.VMEM((2, FFS, HALF), BF16),
-            dma((15,)),
+            dma((18,)),
             pltpu.VMEM((LANES, WAVE, HEADS, 128), F32),
             pltpu.VMEM((2, DEVICES, OWN_HEADS * WAVE, LAT), BF16),
             pltpu.VMEM((2, DEVICES, OWN_HEADS * WAVE, LAT), BF16),

time: 60.6 us -> 60.6 us (level)
  no operation moved by 1% of the time
where the time goes in v4:
time: 60.6 us; the launch traced here: 60.4 us
  Pallas kernels  59 us (97%)
  local copies, waits for them, and re-layouts  1.45 us (2%)
    pallas_call x1, Pallas kernels, shards(): pl.pallas_call(layer_kernel, out_shape=jax.ShapeDtypeStruct((SLOT, D), BF...  59 us
    unnamed x1, local copies, waits for them, and re-layouts  1.45 us

profile of v4, /device:TPU:1, one launch (start us, length us, event | category | flops | bytes accessed | tf_op | source)
XLA Modules:
  0.0 60.4 jit_solution(9843501091855321114)
XLA Ops:
  0.0 59.0 %shard_map.109 = bf16[8,3584]{1,0:T(8,128)(2,1)} custom-call(s32[8]{0:T(128)} %lengths_hbm.1, s32[8]{0:T(128)} %occupied_hbm.1, bf16[8,576,128]{2,1,0:T(8,128)(2,1)} %bitcast.8, bf16[8,576,384]{2,1,0:T(8,128)(2,1)} %bitcast.5, bf16[4,512,128]{2,1,0:T(8,128)(2,1)} %w_uv.1, bf16[512,3584]{1,0:T(8,128)(2,1)} %w_out.1, bf16[288,3584]{1,0:T(8,128)(2,1)} %bitcast.6, ...), custom_call_target="tpu_custom_call" | custom-call | flops 3600000000 | bytes 15000000 | tf_op jit(solution)/shard_map/pallas_call | solution.py:392
  59.0 1.4 %copy.13 = bf16[8,3584]{1,0:T(8,128)(2,1)} copy(bf16[8,3584]{1,0:T(8,128)(2,1)} %shard_map.109) | data formatting | bytes 114688

commit v5 on v4

--- a/solution.py
+++ b/solution.py
@@ -217,7 +217,6 @@
     def project(w):
         others = a2a_in.at[w, pl.ds(0, DEVICES - 1)]
         wait_bytes(others, a2a_recv.at[w])
-        wait_bytes(others, a2a_send.at[w])
         product = jnp.dot(
             a2a_in[w].reshape(DEVICES * OWN_HEADS * WAVE, LAT),
             uv_v[...],
@@ -249,7 +248,6 @@
     def sum_end(n, w):
         m = 2 * n + w
         wait_bytes(rd.at[m], rd_recv.at[m])
-        wait_bytes(rd.at[m], rd_send.at[m])
         total = acc[w, y, x]
         for i in range(CHIPS - 1):
             total += rd[m, i].astype(F32)
@@ -299,7 +297,6 @@
 
     def expand(w):
         wait_bytes(gathered.at[w, 1 - core], swap_recv.at[w])
-        wait_bytes(gathered.at[w, 1 - core], swap_send.at[w])
         up = up_own[w] + wide(w, 1 - core)
         gate = up[:FFS]
         acts[w, core] = (gate / (1.0 + jnp.exp(-gate)) * up[FFS:]).astype(BF16)
@@ -376,6 +373,10 @@
     last = remote(last_own.at[1 - core], last_in, pair_send.at[3], pair_recv.at[3], partner)
     last.start()
     for w in range(2):
+        wait_bytes(a2a_in.at[w, pl.ds(0, DEVICES - 1)], a2a_send.at[w])
+        wait_bytes(rd.at[w], rd_send.at[w])
+        wait_bytes(rd.at[2 + w], rd_send.at[2 + w])
+        wait_bytes(gathered.at[w, core], swap_send.at[w])
         wait_bytes(gathered.at[w, core, pl.ds(0, SIDE - 1)], ag_send.at[w])
         wait_bytes(gathered.at[w, core, 0, pl.ds(0, SIDE - 1)], ag_send.at[w])
     last.wait()

time: 60.6 us -> 60.6 us (level)
  no operation moved by 1% of the time
where the time goes in v5:
time: 60.6 us; the launch traced here: 60.5 us
  Pallas kernels  59 us (97%)
  local copies, waits for them, and re-layouts  1.45 us (2%)
    pallas_call x1, Pallas kernels, shards(): pl.pallas_call(layer_kernel, out_shape=jax.ShapeDtypeStruct((SLOT, D), BF...  59 us
    unnamed x1, local copies, waits for them, and re-layouts  1.45 us

profile of v5, /device:TPU:1, one launch (start us, length us, event | category | flops | bytes accessed | tf_op | source)
XLA Modules:
  0.0 60.5 jit_solution(14994497775464153805)
XLA Ops:
  0.0 59.0 %shard_map.109 = bf16[8,3584]{1,0:T(8,128)(2,1)} custom-call(s32[8]{0:T(128)} %lengths_hbm.1, s32[8]{0:T(128)} %occupied_hbm.1, bf16[8,576,128]{2,1,0:T(8,128)(2,1)} %bitcast.8, bf16[8,576,384]{2,1,0:T(8,128)(2,1)} %bitcast.5, bf16[4,512,128]{2,1,0:T(8,128)(2,1)} %w_uv.1, bf16[512,3584]{1,0:T(8,128)(2,1)} %w_out.1, bf16[288,3584]{1,0:T(8,128)(2,1)} %bitcast.6, ...), custom_call_target="tpu_custom_call" | custom-call | flops 3600000000 | bytes 15000000 | tf_op jit(solution)/shard_map/pallas_call | solution.py:393
  59.0 1.4 %copy.13 = bf16[8,3584]{1,0:T(8,128)(2,1)} copy(bf16[8,3584]{1,0:T(8,128)(2,1)} %shard_map.109) | data formatting | bytes 114688
